TPU v7x, 32 devices: a whole 2x2x4 slice. The times are simulated.
32 devices in a mesh: row: 4 (over y, x), col: 8 (over z, core).
Axes of the slice: x: 2, y: 2, z: 4, core: 2. Of those that a mesh axis runs over, the one named last changes fastest.
Arguments:
- state: float32 [3072, 3072], P('col', 'row'), may hold values from -300 to 300
- noise: float32 [3072, 3072], P('col', 'row'), may hold values from -6 to 6
- mod_shift: float32 [3072], P('col'), may hold values from -3 to 3
- mod_scale: float32 [3072], P('col'), may hold values from -2.5 to 2.5
- mod_gate: float32 [3072], P('col'), may hold values from 0.3 to 3
- w_in: bfloat16 [3072, 12288], P('row', 'col'), may hold values from -0.109375 to 0.109375
- b_in: float32 [12288], P('col'), may hold values from -3 to 3
- w_out: bfloat16 [3072, 12288], P('col', 'row'), may hold values from -0.0546875 to 0.0546875
- b_out: float32 [3072], P('col'), may hold values from -2.5 to 2.5
Outputs:
- purified: float32 [3072, 3072], P('col', 'row')
- predicted: float32 [3072, 3072], P('col', 'row')
All inputs are finite; a program needn't handle non-finite values.
Results may differ from a plain program's by a relative error of at most 0.00049.
Values may be sent and summed in bfloat16 or wider, within the bound.
A program may use at most 128 MiB of HBM per device.

v0:
```python
import math
import jax
import jax.numpy as jnp
from jax import lax
from jax.sharding import PartitionSpec as P

D = 3072
beta_now = 2.09
step_width = 0.02
sigma_now = 0.322


def on_device(state, noise, mod_shift, mod_scale, mod_gate, w_in, b_in, w_out, b_out):
    w_in_all = lax.all_gather(w_in, "row", axis=0, tiled=True)
    w_out_all = lax.all_gather(w_out, "row", axis=1, tiled=True)
    col_sums, squares = lax.psum((jnp.sum(state, axis=0), jnp.sum(state * state, axis=0)), "col")
    center = col_sums / D
    spread = squares / D - center * center
    normed = (
        (state - center[None, :]) * lax.rsqrt(spread[None, :] + 1e-06) * (1.0 + mod_scale[:, None])
        + mod_shift[:, None]
    ).astype(jnp.bfloat16)
    normed_all = lax.all_gather(normed, "col", axis=0, tiled=True)
    pre_act = lax.dot_general(
        w_in_all, normed_all, (((0,), (0,)), ((), ())), preferred_element_type=jnp.float32
    )
    hidden = jax.nn.gelu(pre_act + b_in[:, None], approximate=True).astype(jnp.bfloat16)
    hidden_all = lax.all_gather(hidden, "col", axis=0, tiled=True)
    mixed_out = jnp.dot(w_out_all, hidden_all, preferred_element_type=jnp.float32)
    branch = mixed_out + b_out[:, None]
    predicted = state + mod_gate[:, None] * branch
    purified = (
        state * (1.0 + 0.5 * beta_now * step_width)
        - beta_now * step_width / sigma_now * predicted
        + math.sqrt(beta_now * step_width) * noise
    )
    return (purified, predicted)


def solution(mesh):
    in_specs = (
        P("col", "row"),
        P("col", "row"),
        P("col"),
        P("col"),
        P("col"),
        P("row", "col"),
        P("col"),
        P("col", "row"),
        P("col"),
    )
    out_specs = (P("col", "row"), P("col", "row"))
    return jax.shard_map(
        on_device, mesh=mesh, in_specs=in_specs, out_specs=out_specs, check_vma=False
    )
```

profile of v0, /device:TPU:0, one launch (start us, length us, event | category | flops | bytes accessed | tf_op | source)
XLA Modules:
  0.0 473.4 jit_solution(9994325539912814488)
XLA Ops:
  7.2 0.0 all-gather.5.cloned.1.call-start
  7.2 0.7 broadcast_add_fusion
  7.9 1.4 fusion.11
  9.3 18.3 %all-reduce = (f32[768]{0:T(1024)S(1)}, f32[768]{0:T(1024)S(1)}) all-reduce(f32[768]{0:T(1024)S(1)} %get-tuple-element.5, f32[768]{0:T(1024)S(1)} %get-tuple-element.4), channel_id=1, replica_groups=mesh['row'=4,'col'=8] {'col'}, use_global_device_ids=true, to_apply=%region_3.0 | all-reduce | flops 1536 | bytes 12288 | tf_op jit(solution)/shard_map/psum | solution.py:16
  27.7 2.3 add_convert_fusion
  29.9 0.0 all-gather.5.cloned.1.call-update
  30.0 0.0 copy-start.2
  30.0 0.0 all-gather.7.cloned.1.call-start
  30.0 0.7 all-gather.7.cloned.1.call-update
  30.7 0.0 all-gather.11.cloned.1.call-start
  30.8 0.7 all-gather.11.cloned.1.call-update
  31.5 0.0 all-gather.9.cloned.1.call-start
  31.5 48.5 %all-gather.5.cloned.1.call-done = bf16[3072,768]{1,0:T(8,128)(2,1)} async-done(((bf16[384,768]{1,0:T(8,128)(2,1)}), bf16[3072,768]{1,0:T(8,128)(2,1)}) %all-gather.5.cloned.1.call-update) | async-done | bytes 4718608 | tf_op jit(solution)/shard_map/all_gather | solution.py:23
  80.1 97.0 %all-gather.7.cloned.1.call-done = bf16[3072,1536]{1,0:T(8,128)(2,1)} async-done(((bf16[768,1536]{1,0:T(8,128)(2,1)}), bf16[3072,1536]{1,0:T(8,128)(2,1)}) %all-gather.7.cloned.1.call-update) | async-done | bytes 9437200 | tf_op jit(solution)/shard_map/all_gather | solution.py:14
  177.1 0.0 copy-done.2
  177.1 13.7 %fusion.7 = bf16[1536,768]{0,1:T(8,128)(2,1)} fusion(bf16[3072,768]{1,0:T(8,128)(2,1)} %all-gather.5.cloned.1.call-done, bf16[3072,1536]{1,0:T(8,128)(2,1)} %all-gather.7.cloned.1.call-done, f32[1536]{0:T(1024)S(1)} %copy-done.2), kind=kOutput, calls=%fused_computation.8 | convolution fusion | flops 7259553792 | bytes 16521216 | tf_op jit(solution)/shard_map/dot_general | solution.py:24
  190.7 0.0 copy-start
  190.7 0.0 copy-start.1
  190.7 0.0 all-gather.9.cloned.1.call-update
  190.8 1.3 copy-done
  192.1 0.0 copy-start.3
  192.1 0.0 copy-start.4
  192.1 0.4 copy.11
  192.5 0.0 copy-done.1
  192.5 0.4 copy.13
  192.9 82.4 %all-gather.11.cloned.1.call-done = bf16[384,12288]{1,0:T(8,128)(2,1)} async-done(((bf16[384,3072]{1,0:T(8,128)(2,1)}), bf16[384,12288]{1,0:T(8,128)(2,1)}) %all-gather.11.cloned.1.call-update) | async-done | bytes 9437200 | tf_op jit(solution)/shard_map/all_gather | solution.py:15
  275.3 169.8 %all-gather.9.cloned.1.call-done = bf16[12288,768]{0,1:T(8,128)(2,1)} async-done(((bf16[1536,768]{0,1:T(8,128)(2,1)}), bf16[12288,768]{0,1:T(8,128)(2,1)}) %all-gather.9.cloned.1.call-update) | async-done | bytes 18874384 | tf_op jit(solution)/shard_map/all_gather | solution.py:28
  445.1 0.0 copy-done.3
  445.1 0.0 copy-done.4
  445.1 17.8 %multiply_add_fusion = (f32[384,768]{0,1:T(8,128)}, f32[384,768]{0,1:T(8,128)S(1)}) fusion(f32[384,768]{0,1:T(8,128)S(1)} %copy.13, f32[384,768]{0,1:T(8,128)S(1)} %copy.11, f32[384]{0:T(512)S(1)} %copy-done.3, bf16[12288,768]{0,1:T(8,128)(2,1)} %all-gather.9.cloned.1.call-done, bf16[384,12288]{1,0:T(8,128)(2,1)} %all-gather.11.cloned.1.call-done, ...), kind=kOutput, calls=%fused_computation.13 | convolution fusion | flops 7250116608 | bytes 33033216 | tf_op jit(solution)/shard_map/dot_general | solution.py:29
  462.8 2.7 copy.14
  465.5 1.4 copy.15
  (1 shorter events, 0.0 us)
Async XLA Ops:
  7.2 72.9 %all-gather.5.cloned.1.call-start = ((), (), s32[]{:S(2)}) async-start(), calls=%async_computation | async-start | bytes 5308416 | tf_op jit(solution)/shard_map/all_gather | solution.py:23
  30.0 147.1 %copy-start.2 = (f32[1536]{0:T(1024)S(1)}, f32[1536]{0:T(1024)}, u32[]{:S(2)}) copy-start(f32[1536]{0:T(1024)} %param.15) | copy-start | bytes 18436
  30.0 147.1 %all-gather.7.cloned.1.call-start = ((), (), s32[]{:S(2)}) async-start(), calls=%async_computation.1 | async-start | bytes 11796480 | tf_op jit(solution)/shard_map/all_gather | solution.py:14
  30.7 244.6 %all-gather.11.cloned.1.call-start = ((), (), s32[]{:S(2)}) async-start(), calls=%async_computation.3 | async-start | bytes 11796480 | tf_op jit(solution)/shard_map/all_gather | solution.py:15
  31.5 413.6 %all-gather.9.cloned.1.call-start = ((), (), s32[]{:S(2)}) async-start(), calls=%async_computation.2 | async-start | bytes 21233664 | tf_op jit(solution)/shard_map/all_gather | solution.py:28
  190.7 1.4 copy-start
  190.7 1.8 copy-start.1
  192.1 253.0 %copy-start.3 = (f32[384]{0:T(512)S(1)}, f32[384]{0:T(512)}, u32[]{:S(2)}) copy-start(f32[384]{0:T(512)} %param.17) | copy-start | bytes 4612
  192.1 253.0 %copy-start.4 = (f32[384]{0:T(512)S(1)}, f32[384]{0:T(512)}, u32[]{:S(2)}) copy-start(f32[384]{0:T(512)} %param.13) | copy-start | bytes 4612
Sparse Core Ops, SparseCore 0:
  30.1 49.9 all-gather.4
  81.9 95.1 all-gather.6
  178.9 96.3 all-gather.10
  276.8 168.2 all-gather.8
where the time goes:
time: 474 us; the launch traced here: 473 us
  waiting for transfers between devices  399 us (84%)
  matrix products  31.4 us (7%)
  blocking collectives  18.3 us (4%)
  between operations  13.8 us (3%)
  local copies, waits for them, and re-layouts  6.13 us (1%)
    all_gather x1, waiting for transfers between devices, on_device(): hidden_all = lax.all_gather(hidden, 'col', axis=0, tiled=True)  170 us
    all_gather x1, waiting for transfers between devices, on_device(): w_in_all = lax.all_gather(w_in, 'row', axis=0, tiled=True)  97 us
    all_gather x1, waiting for transfers between devices, on_device(): w_out_all = lax.all_gather(w_out, 'row', axis=1, tiled=True)  82.4 us
    all_gather x1, waiting for transfers between devices, on_device(): normed_all = lax.all_gather(normed, 'col', axis=0, tiled=True)  48.5 us
    psum x1, blocking collectives, on_device(): lax.psum((jnp.sum(state, axis=0), jnp.sum(state * state, axis=0)), 'col')  18.3 us
    dot_general x1, matrix products, on_device(): jnp.dot(w_out_all, hidden_all, preferred_element_type=jnp.float32)  17.8 us
    dot_general x1, matrix products, on_device(): lax.dot_general(w_in_all, normed_all, (((0,), (0,)), ((), ())), preferred...  13.7 us
  transfers between devices with their start and end apart: 4, of which 4 were waited for; matrix products, arithmetic and copies ran while one was open for 3% of the time, Pallas kernels for 0%

commit v1 on v0

--- a/solution.py
+++ b/solution.py
@@ -25,7 +25,21 @@
         w_in_all, normed_all, (((0,), (0,)), ((), ())), preferred_element_type=jnp.float32
     )
     hidden = jax.nn.gelu(pre_act + b_in[:, None], approximate=True).astype(jnp.bfloat16)
-    hidden_all = lax.all_gather(hidden, "col", axis=0, tiled=True)
+    ways, here, step = (lax.axis_size("col"), lax.axis_index("col"), hidden.shape[0])
+    dims = [n * ways if d == 0 else n for d, n in enumerate(hidden.shape)]
+    full = lax.dynamic_update_slice_in_dim(
+        jnp.zeros(dims, hidden.dtype), hidden, here * step, axis=0
+    )
+    going_up = going_down = hidden
+    for far in range(1, ways // 2 + 1):
+        going_up = lax.ppermute(going_up, "col", [(d, (d + 1) % ways) for d in range(ways)])
+        full = lax.dynamic_update_slice_in_dim(full, going_up, (here - far) % ways * step, axis=0)
+        if 2 * far < ways:
+            going_down = lax.ppermute(going_down, "col", [(d, (d - 1) % ways) for d in range(ways)])
+            full = lax.dynamic_update_slice_in_dim(
+                full, going_down, (here + far) % ways * step, axis=0
+            )
+    hidden_all = full
     mixed_out = jnp.dot(w_out_all, hidden_all, preferred_element_type=jnp.float32)
     branch = mixed_out + b_out[:, None]
     predicted = state + mod_gate[:, None] * branch

time: 474 us -> 425 us (0.90)
  waiting for transfers between devices: 399 us -> 311 us
  local copies, waits for them, and re-layouts: 6.13 us -> 39.6 us
  starting transfers between devices: 0.16 us -> 9.38 us
    all_gather x1 -> x0, waiting for transfers between devices: 170 us -> none  [on_device(): hidden_all = lax.all_gather(hidden, 'col', axis=0, tiled=True)]
    ppermute x0 -> x7, waiting for transfers between devices: none -> 164 us  [the longest x4 164 us: on_device(): lax.ppermute(going_up, 'col', [(d, (d + 1) % ways) for d in range(ways)])]
    all_gather x1, waiting for transfers between devices: 82.4 us -> 0.01 us  [on_device(): w_out_all = lax.all_gather(w_out, 'row', axis=1, tiled=True)]
    dynamic_update_slice x0 -> x7, local copies, waits for them, and re-layouts: none -> 18 us  [the longest x4 9.75 us: on_device(): lax.dynamic_update_slice_in_dim(full, going_up, (here - far) % ways * ste...]
    broadcast_in_dim x0 -> x1, local copies, waits for them, and re-layouts: none -> 9.5 us  [on_device(): jnp.zeros(dims, hidden.dtype)]
    ppermute x0 -> x7, starting transfers between devices: none -> 9.26 us  [the longest x3 9.25 us: on_device(): lax.ppermute(going_down, 'col', [(d, (d - 1) % ways) for d in range(ways)])]
    unnamed x14 -> x26, local copies, waits for them, and re-layouts: 6.13 us -> 12.1 us
  transfers between devices with their start and end apart: 4 -> 10, of which waited for: 4 -> 6; matrix products, arithmetic and copies ran while one was open for 3% -> 10% of each run, Pallas kernels for 0% -> 0%
where the time goes in v1:
time: 425 us; the launch traced here: 424 us
  waiting for transfers between devices  311 us (73%)
  local copies, waits for them, and re-layouts  39.6 us (9%)
  matrix products  27.9 us (7%)
  blocking collectives  18.3 us (4%)
  between operations  13.9 us (3%)
  starting transfers between devices  9.38 us (2%)
  other arithmetic  4.4 us (1%)
    ppermute x4, waiting for transfers between devices, on_device(): lax.ppermute(going_up, 'col', [(d, (d + 1) % ways) for d in range(ways)])  164 us
    all_gather x1, waiting for transfers between devices, on_device(): w_in_all = lax.all_gather(w_in, 'row', axis=0, tiled=True)  97 us
    all_gather x1, waiting for transfers between devices, on_device(): normed_all = lax.all_gather(normed, 'col', axis=0, tiled=True)  48.6 us
    psum x1, blocking collectives, on_device(): lax.psum((jnp.sum(state, axis=0), jnp.sum(state * state, axis=0)), 'col')  18.3 us
    dot_general x1, matrix products, on_device(): jnp.dot(w_out_all, hidden_all, preferred_element_type=jnp.float32)  17.8 us
    unnamed x26, local copies, waits for them, and re-layouts  12.1 us
    dot_general x1, matrix products, on_device(): lax.dot_general(w_in_all, normed_all, (((0,), (0,)), ((), ())), preferred...  10.1 us
    dynamic_update_slice x4, local copies, waits for them, and re-layouts, on_device(): lax.dynamic_update_slice_in_dim(full, going_up, (here - far) % ways * ste...  9.75 us
  transfers between devices with their start and end apart: 10, of which 6 were waited for; matrix products, arithmetic and copies ran while one was open for 10% of the time, Pallas kernels for 0%

profile of v1, /device:TPU:0, one launch (start us, length us, event | category | flops | bytes accessed | tf_op | source)
XLA Modules:
  0.0 424.5 jit_solution(5247592433749182382)
XLA Ops:
  7.2 0.0 all-gather.4.cloned.1.call-start
  7.2 1.4 fusion.11
  8.6 0.7 broadcast_add_fusion
  9.3 18.3 %all-reduce = (f32[768]{0:T(1024)S(1)}, f32[768]{0:T(1024)S(1)}) all-reduce(f32[768]{0:T(1024)S(1)} %get-tuple-element.5, f32[768]{0:T(1024)S(1)} %get-tuple-element.4), channel_id=1, replica_groups=mesh['row'=4,'col'=8] {'col'}, use_global_device_ids=true, to_apply=%region_3.0 | all-reduce | flops 1536 | bytes 12288 | tf_op jit(solution)/shard_map/psum | solution.py:16
  27.6 2.3 add_convert_fusion
  29.9 0.0 all-gather.4.cloned.1.call-update
  30.0 0.0 all-gather.6.cloned.1.call-start
  30.0 0.7 all-gather.6.cloned.1.call-update
  30.7 0.0 all-gather.8.cloned.1.call-start
  30.7 0.7 all-gather.8.cloned.1.call-update
  31.4 0.0 copy-start.8
  31.5 48.6 %all-gather.4.cloned.1.call-done = bf16[3072,768]{1,0:T(8,128)(2,1)} async-done(((bf16[384,768]{1,0:T(8,128)(2,1)}), bf16[3072,768]{1,0:T(8,128)(2,1)}) %all-gather.4.cloned.1.call-update) | async-done | bytes 4718608 | tf_op jit(solution)/shard_map/all_gather | solution.py:23
  80.0 97.0 %all-gather.6.cloned.1.call-done = bf16[3072,1536]{1,0:T(8,128)(2,1)} async-done(((bf16[768,1536]{1,0:T(8,128)(2,1)}), bf16[3072,1536]{1,0:T(8,128)(2,1)}) %all-gather.6.cloned.1.call-update) | async-done | bytes 9437200 | tf_op jit(solution)/shard_map/all_gather | solution.py:14
  177.0 0.0 copy-start.6
  177.0 0.0 copy-start.7
  177.1 9.5 %broadcast_in_dim.2 = bf16[12288,768]{0,1:T(8,128)(2,1)} broadcast(bf16[]{:T(256)} %constant.63.clone.1), dimensions={} | broadcast | bytes 18874370 | tf_op jit(solution)/shard_map/broadcast_in_dim | solution.py:31
  186.6 0.0 copy-done.8
  186.6 0.0 copy-done.6
  186.6 2.7 copy-done.7
  189.3 0.0 copy-start
  189.3 10.1 %constant_dynamic-update-slice_fusion.7 = (bf16[12288,768]{0,1:T(8,128)(2,1)}, bf16[1536,768]{0,1:T(8,128)(2,1)S(1)}) fusion(bf16[12288,768]{0,1:T(8,128)(2,1)} %broadcast_in_dim.2, s32[]{:T(128)S(6)} %select_n.55, f32[1536]{0:T(1024)S(1)} %copy-done.8, bf16[3072,768]{1,0:T(8,128)(2,1)S(1)} %copy-done.7, bf16[3072,1536]{1,0:T(8,128)(2,1)S(1)} %copy-done.6), kind=kOutput, calls=%fused_computation.24 | convolution fusion | flops 7259553792 | bytes 18880516 | tf_op jit(solution)/shard_map/dot_general | solution.py:24
  199.4 0.0 collective-permute-start
  199.4 3.5 collective-permute-start.1
  202.9 49.9 %collective-permute-done = bf16[1536,768]{0,1:T(8,128)(2,1)S(1)} collective-permute-done((bf16[1536,768]{0,1:T(8,128)(2,1)S(1)}, bf16[1536,768]{0,1:T(8,128)(2,1)S(1)}, u32[]{:S(2)}, u32[]{:S(2)}) %collective-permute-start) | collective-permute-done | bytes 2359328 | tf_op jit(solution)/shard_map/ppermute | solution.py:35
  252.8 0.0 collective-permute-start.2
  252.8 0.0 collective-permute-done.1
  252.8 0.0 copy-start.1
  252.8 3.5 collective-permute-start.3
  256.4 51.4 %collective-permute-done.2 = bf16[1536,768]{0,1:T(8,128)(2,1)S(1)} collective-permute-done((bf16[1536,768]{0,1:T(8,128)(2,1)S(1)}, bf16[1536,768]{0,1:T(8,128)(2,1)S(1)}, u32[]{:S(2)}, u32[]{:S(2)}) %collective-permute-start.2) | collective-permute-done | bytes 2359328 | tf_op jit(solution)/shard_map/ppermute | solution.py:35
  307.7 0.0 copy-done.1
  307.7 0.0 copy-start.3
  307.8 0.0 collective-permute-start.4
  307.8 0.0 collective-permute-done.3
  307.8 1.4 copy-done.3
  309.1 2.2 collective-permute-start.5
  311.3 51.1 %collective-permute-done.4 = bf16[1536,768]{0,1:T(8,128)(2,1)} collective-permute-done((bf16[1536,768]{0,1:T(8,128)(2,1)S(1)}, bf16[1536,768]{0,1:T(8,128)(2,1)}, u32[]{:S(2)}, u32[]{:S(2)}) %collective-permute-start.4) | collective-permute-done | bytes 2359328 | tf_op jit(solution)/shard_map/ppermute | solution.py:35
  362.4 0.0 collective-permute-start.6
  362.5 0.0 copy-done
  362.5 1.4 copy.11
  363.8 1.6 copy.13
  365.5 0.0 copy-start.2
  365.5 0.0 copy-start.4
  365.5 1.6 constant_dynamic-update-slice_fusion.6
  367.1 0.9 copy-done.2
  368.0 1.6 constant_dynamic-update-slice_fusion.5
  369.7 0.0 copy-done.4
  369.7 1.6 constant_dynamic-update-slice_fusion.4
  371.3 3.3 constant_dynamic-update-slice_fusion.3
  374.6 3.3 constant_dynamic-update-slice_fusion.2
  377.8 0.0 copy-start.5
  377.8 0.0 copy-start.9
  377.9 0.0 copy-start.10
  377.9 0.0 collective-permute-done.5
  377.9 3.3 constant_dynamic-update-slice_fusion.1
  381.2 11.6 %collective-permute-done.6 = bf16[1536,768]{0,1:T(8,128)(2,1)} collective-permute-done((bf16[1536,768]{0,1:T(8,128)(2,1)}, bf16[1536,768]{0,1:T(8,128)(2,1)}, u32[]{:S(2)}, u32[]{:S(2)}) %collective-permute-start.6) | collective-permute-done | bytes 2359328 | tf_op jit(solution)/shard_map/ppermute | solution.py:35
  392.8 3.3 constant_dynamic-update-slice_fusion
  396.1 0.0 all-gather.8.cloned.1.call-done
  396.1 0.0 copy-done.5
  396.1 0.0 copy-done.9
  396.1 0.0 copy-done.10
  396.1 17.8 %multiply_add_fusion = (f32[384,768]{0,1:T(8,128)}, f32[384,768]{0,1:T(8,128)S(1)}) fusion(f32[384,768]{0,1:T(8,128)S(1)} %copy.13, f32[384,768]{0,1:T(8,128)S(1)} %copy-done.5, f32[384]{0:T(512)S(1)} %copy-done.9, bf16[12288,768]{0,1:T(8,128)(2,1)} %constant_dynamic-update-slice_fusion, bf16[384,12288]{1,0:T(8,128)(2,1)} %all-gather.8.cloned.1.call-done, ...), kind=kOutput, calls=%fused_computation.13 | convolution fusion | flops 7250116608 | bytes 33033216 | tf_op jit(solution)/shard_map/dot_general | solution.py:43
  413.9 2.7 copy.14
  416.6 1.4 copy.15
  (1 shorter events, 0.0 us)
Async XLA Ops:
  7.2 72.9 %all-gather.4.cloned.1.call-start = ((), (), s32[]{:S(2)}) async-start(), calls=%async_computation | async-start | bytes 5308416 | tf_op jit(solution)/shard_map/all_gather | solution.py:23
  30.0 147.1 %all-gather.6.cloned.1.call-start = ((), (), s32[]{:S(2)}) async-start(), calls=%async_computation.1 | async-start | bytes 11796480 | tf_op jit(solution)/shard_map/all_gather | solution.py:14
  30.7 365.4 %all-gather.8.cloned.1.call-start = ((), (), s32[]{:S(2)}) async-start(), calls=%async_computation.2 | async-start | bytes 11796480 | tf_op jit(solution)/shard_map/all_gather | solution.py:15
  31.4 155.1 %copy-start.8 = (f32[1536]{0:T(1024)S(1)}, f32[1536]{0:T(1024)}, u32[]{:S(2)}) copy-start(f32[1536]{0:T(1024)} %param.15) | copy-start | bytes 18436
  177.0 9.5 %copy-start.6 = (bf16[3072,1536]{1,0:T(8,128)(2,1)S(1)}, bf16[3072,1536]{1,0:T(8,128)(2,1)}, u32[]{:S(2)}) copy-start(bf16[3072,1536]{1,0:T(8,128)(2,1)} %all-gather.6.cloned.1.call-done) | copy-start | bytes 28311556
  177.0 12.2 %copy-start.7 = (bf16[3072,768]{1,0:T(8,128)(2,1)S(1)}, bf16[3072,768]{1,0:T(8,128)(2,1)}, u32[]{:S(2)}) copy-start(bf16[3072,768]{1,0:T(8,128)(2,1)} %all-gather.4.cloned.1.call-done) | copy-start | bytes 14155780
  189.3 173.2 %copy-start = (f32[384,768]{1,0:T(8,128)S(1)}, f32[384,768]{1,0:T(8,128)}, u32[]{:S(2)}) copy-start(f32[384,768]{1,0:T(8,128)} %param.9) | copy-start | bytes 3538948
  199.4 53.4 %collective-permute-start = (bf16[1536,768]{0,1:T(8,128)(2,1)S(1)}, bf16[1536,768]{0,1:T(8,128)(2,1)S(1)}, u32[]{:S(2)}, u32[]{:S(2)}) collective-permute-start(bf16[1536,768]{0,1:T(8,128)(2,1)S(1)} %get-tuple-element.11), channel_id=1, source_target_pairs={{0,1},{1,2},{2,3},{3,4},{4,5},{5,6},{6,7},{7,0},{8,9},{9,10},{10,1... | collective-permute-start | bytes 7077896 | tf_op jit(solution)/shard_map/ppermute | solution.py:35
  199.4 53.5 %collective-permute-start.1 = (bf16[1536,768]{0,1:T(8,128)(2,1)S(1)}, bf16[1536,768]{0,1:T(8,128)(2,1)S(1)}, u32[]{:S(2)}, u32[]{:S(2)}) collective-permute-start(bf16[1536,768]{0,1:T(8,128)(2,1)S(1)} %get-tuple-element.11), channel_id=1, source_target_pairs={{0,7},{1,0},{2,1},{3,2},{4,3},{5,4},{6,5},{7,6},{8,15},{9,8},{10,9... | collective-permute-start | bytes 7077896 | tf_op jit(solution)/shard_map/ppermute | solution.py:38
  252.8 54.9 %collective-permute-start.2 = (bf16[1536,768]{0,1:T(8,128)(2,1)S(1)}, bf16[1536,768]{0,1:T(8,128)(2,1)S(1)}, u32[]{:S(2)}, u32[]{:S(2)}) collective-permute-start(bf16[1536,768]{0,1:T(8,128)(2,1)S(1)} %collective-permute-done), channel_id=1, source_target_pairs={{0,1},{1,2},{2,3},{3,4},{4,5},{5,6},{6,7},{7,0},{8,9},{9,10},{10,1... | collective-permute-start | bytes 7077896 | tf_op jit(solution)/shard_map/ppermute | solution.py:35
  252.8 54.9 %copy-start.1 = (bf16[1536,768]{0,1:T(8,128)(2,1)}, bf16[1536,768]{0,1:T(8,128)(2,1)S(1)}, u32[]{:S(2)}) copy-start(bf16[1536,768]{0,1:T(8,128)(2,1)S(1)} %collective-permute-done.1) | copy-start | bytes 7077892
  252.8 54.9 %collective-permute-start.3 = (bf16[1536,768]{0,1:T(8,128)(2,1)S(1)}, bf16[1536,768]{0,1:T(8,128)(2,1)}, u32[]{:S(2)}, u32[]{:S(2)}) collective-permute-start(bf16[1536,768]{0,1:T(8,128)(2,1)S(1)} %collective-permute-done.1), channel_id=1, source_target_pairs={{0,7},{1,0},{2,1},{3,2},{4,3},{5,4},{6,5},{7,6},{8,15},{9,8},{10,9... | collective-permute-start | bytes 7077896 | tf_op jit(solution)/shard_map/ppermute | solution.py:38
  307.7 1.4 copy-start.3
  307.8 54.7 %collective-permute-start.4 = (bf16[1536,768]{0,1:T(8,128)(2,1)S(1)}, bf16[1536,768]{0,1:T(8,128)(2,1)}, u32[]{:S(2)}, u32[]{:S(2)}) collective-permute-start(bf16[1536,768]{0,1:T(8,128)(2,1)S(1)} %collective-permute-done.2), channel_id=1, source_target_pairs={{0,1},{1,2},{2,3},{3,4},{4,5},{5,6},{6,7},{7,0},{8,9},{9,10},{10,1... | collective-permute-start | bytes 7077896 | tf_op jit(solution)/shard_map/ppermute | solution.py:35
  309.1 68.7 %collective-permute-start.5 = (bf16[1536,768]{0,1:T(8,128)(2,1)}, bf16[1536,768]{0,1:T(8,128)(2,1)}, u32[]{:S(2)}, u32[]{:S(2)}) collective-permute-start(bf16[1536,768]{0,1:T(8,128)(2,1)} %collective-permute-done.3), channel_id=1, source_target_pairs={{0,7},{1,0},{2,1},{3,2},{4,3},{5,4},{6,5},{7,6},{8,15},{9,8},{10,9... | collective-permute-start | bytes 7077896 | tf_op jit(solution)/shard_map/ppermute | solution.py:38
  362.4 30.4 %collective-permute-start.6 = (bf16[1536,768]{0,1:T(8,128)(2,1)}, bf16[1536,768]{0,1:T(8,128)(2,1)}, u32[]{:S(2)}, u32[]{:S(2)}) collective-permute-start(bf16[1536,768]{0,1:T(8,128)(2,1)} %collective-permute-done.4), channel_id=1, source_target_pairs={{0,1},{1,2},{2,3},{3,4},{4,5},{5,6},{6,7},{7,0},{8,9},{9,10},{10,1... | collective-permute-start | bytes 7077896 | tf_op jit(solution)/shard_map/ppermute | solution.py:35
  365.5 2.5 copy-start.2
  365.5 4.1 copy-start.4
  377.8 18.3 %copy-start.5 = (f32[384,768]{0,1:T(8,128)S(1)}, f32[384,768]{0,1:T(8,128)}, u32[]{:S(2)}) copy-start(f32[384,768]{0,1:T(8,128)} %copy.11) | copy-start | bytes 3538948
  377.8 18.3 %copy-start.9 = (f32[384]{0:T(512)S(1)}, f32[384]{0:T(512)}, u32[]{:S(2)}) copy-start(f32[384]{0:T(512)} %param.17) | copy-start | bytes 4612
  377.9 18.3 %copy-start.10 = (f32[384]{0:T(512)S(1)}, f32[384]{0:T(512)}, u32[]{:S(2)}) copy-start(f32[384]{0:T(512)} %param.13) | copy-start | bytes 4612
Sparse Core Ops, SparseCore 0:
  30.1 49.9 all-gather.3
  81.9 95.1 all-gather.5
  178.9 96.3 all-gather.7
